TPU v7x, 256 devices: a whole 4x4x8 slice. The times are simulated.
256 devices in a mesh: blk: 32 (over y_hi, z, core), head: 8 (over x, y_lo).
Axes of the slice: x: 4, y: 4 (y_hi: 2, y_lo: 2; y = y_hi * 2 + y_lo), z: 8, core: 2. Of those that a mesh axis runs over, the one named last changes fastest.
Arguments:
- queries: bfloat16 [2048, 128, 128], P('blk', 'head'), may hold values from -8 to 8
- new_keys: bfloat16 [2048, 8, 128], P('blk', 'head'), may hold values from -12 to 12
- new_values: bfloat16 [2048, 8, 128], P('blk', 'head'), may hold values from -16 to 16
- segment_ids: int32 [2048], P('blk'), may hold values from 0 to 7, never falling along the last dimension, each value on 1 to 1088 neighbouring positions
- cache_keys: bfloat16 [8192, 8, 128], P('blk', 'head'), may hold values from -8 to 8
- cache_values: bfloat16 [8192, 8, 128], P('blk', 'head'), may hold values from -6 to 6
- cache_lengths: int32 [32], P('blk'), may hold values from 1 to 256, 6144 in all
- o_weight: bfloat16 [16384, 16384], P('head', 'blk'), may hold values from -0.046875 to 0.046875
Outputs:
- attended: bfloat16 [2048, 128, 128], P('blk', 'head')
- projected: bfloat16 [2048, 16384], P('head', 'blk')
Inputs may be any that keep to these rules, and one draw needn't show every extreme that they name: `cache_lengths`: the lengths sum to 6144 and the largest is 256. `segment_ids`: never falling along the tokens; each request holds 1 to 1088 tokens, one exactly 1088.
All inputs are finite; a program needn't handle non-finite values. No bound on the sum of `cache_lengths` on one device may be relied on, other than what follows from the above.
Results may differ from a plain program's by a relative error of at most 0.019.
Values may be sent and summed in bfloat16 or wider, within the bound.
A program may use at most 128 MiB of HBM per device.

v0:
```python
import math

import jax
import jax.numpy as jnp
from jax import lax
from jax.sharding import PartitionSpec as P


def block_partial(query_block, key_block, value_block, visible):
    inverse_root = 1.0 / math.sqrt(query_block.shape[-1])
    scores = (
        jnp.einsum("nkgd,ckd->nkgc", query_block, key_block, preferred_element_type=jnp.float32)
        * inverse_root
    )
    scores = jnp.where(visible[:, None, None, :], scores, -jnp.inf)
    highest = jnp.max(scores, axis=-1)
    weights = jnp.exp(scores - highest[..., None]).astype(jnp.bfloat16)
    denominator = jnp.sum(weights.astype(jnp.float32), axis=-1)
    numerator = jnp.einsum(
        "nkgc,ckd->nkgd", weights, value_block, preferred_element_type=jnp.float32
    )
    return (highest, denominator, numerator)


def combine_many(state, highs, denominators, numerators):
    joint = jnp.maximum(state[0], jnp.max(highs, axis=0))
    older = jnp.exp(state[0] - joint)
    newer = jnp.exp(highs - joint)
    denominator = older * state[1] + jnp.sum(newer * denominators, axis=0)
    numerator = older[..., None] * state[2] + jnp.sum(newer[..., None] * numerators, axis=0)
    return (joint, denominator, numerator)


def per_device(
    queries, new_keys, new_values, segment_ids, cache_keys, cache_values, cache_lengths, o_weight
):
    q_dev, heads, width = queries.shape
    kv_local = new_keys.shape[1]
    group = heads // kv_local
    c_dev = cache_keys.shape[0]
    local_queries = queries.reshape(q_dev, kv_local, group, width)
    all_keys, all_values, all_segments = (
        lax.all_gather(new_keys, "blk", axis=0, tiled=True),
        lax.all_gather(new_values, "blk", axis=0, tiled=True),
        lax.all_gather(segment_ids, "blk", axis=0, tiled=True),
    )
    my_rows = lax.axis_index("blk") * q_dev + jnp.arange(q_dev, dtype=jnp.int32)
    key_rows = jnp.arange(all_keys.shape[0], dtype=jnp.int32)
    visible_new = (all_segments[None, :] == segment_ids[:, None]) & (
        key_rows[None, :] <= my_rows[:, None]
    )
    state = block_partial(local_queries, all_keys, all_values, visible_new)
    slot_rows = jnp.arange(c_dev, dtype=jnp.int32)
    key_piece = lax.all_gather(cache_keys, "blk", axis=0, tiled=True)
    value_piece = lax.all_gather(cache_values, "blk", axis=0, tiled=True)
    length_piece = lax.all_gather(cache_lengths, "blk", axis=0, tiled=True)
    shards = length_piece.shape[0]
    key_piece = key_piece.reshape(shards, c_dev, kv_local, width)
    value_piece = value_piece.reshape(shards, c_dev, kv_local, width)

    def single_shard(key_block, value_block, length_value):
        return block_partial(
            local_queries, key_block, value_block, (slot_rows < length_value)[None, :]
        )

    highs, denominators, numerators = jax.vmap(single_shard)(key_piece, value_piece, length_piece)
    state = combine_many(state, highs, denominators, numerators)
    attended = (state[2] / state[1][..., None]).astype(jnp.bfloat16).reshape(q_dev, heads, width)
    flattened = attended.reshape(q_dev, heads * width)
    projection_terms = jnp.dot(
        lax.all_gather(flattened, "blk", axis=0, tiled=True),
        o_weight,
        preferred_element_type=jnp.float32,
    )
    projected = lax.psum_scatter(
        projection_terms.astype(jnp.bfloat16), "head", scatter_dimension=0, tiled=True
    )
    return (attended, projected)


def solution(mesh):
    return jax.shard_map(
        per_device,
        mesh=mesh,
        in_specs=(
            P("blk", "head", None),
            P("blk", "head", None),
            P("blk", "head", None),
            P("blk"),
            P("blk", "head", None),
            P("blk", "head", None),
            P("blk"),
            P("head", "blk"),
        ),
        out_specs=(P("blk", "head", None), P("head", "blk")),
        check_vma=False,
    )
```

profile of v0, /device:TPU:2, one launch (start us, length us, event | category | flops | bytes accessed | tf_op | source)
XLA Modules:
  0.0 355.7 jit_solution(16350765529207425328)
XLA Ops:
  7.2 0.0 copy-start
  7.2 0.0 all-gather.4.cloned.1.call-start
  7.2 0.7 all-gather.4.cloned.1.call-update
  7.9 0.0 all-gather.6.cloned.1.call-start
  8.0 0.7 all-gather.6.cloned.1.call-update
  8.7 0.0 all-gather.8.cloned.1.call-start
  9.4 46.6 %all_gather.22 = bf16[2048,1,128]{2,0,1:T(8,128)(2,1)S(1)} all-gather(bf16[64,1,128]{2,0,1:T(8,128)(2,1)} %param.9), channel_id=1, replica_groups=mesh['blk'=32,'head'=8] {'blk'}, dimensions={0}, use_global_device_ids=true | all-gather | bytes 540672 | tf_op jit(solution)/shard_map/all_gather | solution.py:43
  56.0 38.5 %all_gather.25 = bf16[2048,1,128]{2,0,1:T(8,128)(2,1)S(1)} all-gather(bf16[64,1,128]{2,0,1:T(8,128)(2,1)} %param.10), channel_id=1, replica_groups=mesh['blk'=32,'head'=8] {'blk'}, dimensions={0}, use_global_device_ids=true | all-gather | bytes 540672 | tf_op jit(solution)/shard_map/all_gather | solution.py:44
  94.5 1.3 dynamic-slice
  96.4 0.9 dynamic-update-slice
  97.3 0.8 dynamic-update-slice.1
  98.0 14.9 %all-reduce.2 = (s32[32]{0:T(128)S(1)}, s32[2048]{0:T(1024)S(1)}) all-reduce(s32[32]{0:T(128)S(1)} %dynamic-update-slice.1, s32[2048]{0:T(1024)S(1)} %dynamic-update-slice), channel_id=1, replica_groups=mesh['blk'=32,'head'=8] {'blk'}, use_global_device_ids=true, to_apply=%add.1 | all-reduce | flops 2080 | bytes 16640
  112.9 0.9 fusion.16
  113.8 2.5 fusion.5
  116.3 2.5 convert_reduce_fusion.1
  118.8 0.0 copy-start.1
  118.8 2.7 fusion.6
  121.5 0.1 iota_compare_fusion.1
  121.6 0.0 all-gather.4.cloned.1.call-done
  121.6 0.0 copy-done.1
  121.6 14.8 %bitcast_reduce_fusion = (f32[32,64,16]{1,2,0:T(8,128)S(1)}, f32[32,256,64,16]{1,2,3,0:T(8,128)}) fusion(pred[32,256]{1,0:T(8,128)(4,1)S(1)} %iota_compare_fusion.1, bf16[32,256,128,1]{2,1,3,0:T(8,128)(2,1)} %bitcast.106, bf16[64,16,128]{2,1,0:T(8,128)(2,1)S(1)} %copy-done.1), kind=kOutput, calls=%fused_computation.1 | convolution fusion | flops 2172616704 | bytes 36052992 | tf_op jit(solution)/shard_map/vmap(nkgd,ckd->nkgc)/dot_general | solution.py:12
  136.4 22.7 %convert_reduce_fusion = (f32[32,64,16]{1,2,0:T(8,128)S(1)}, f32[64,16]{0,1:T(8,128)S(1)}, bf16[32,64,16,256]{3,1,2,0:T(8,128)(2,1)}) fusion(f32[32,64,16]{1,2,0:T(8,128)S(1)} %get-tuple-element.11, f32[32,256,64,16]{1,2,3,0:T(8,128)} %get-tuple-element.12, pred[32,256]{1,0:T(8,128)(4,1)S(1)} %iota_compare_fusion.1), kind=kLoop, calls=%fused_computation.6 | loop fusion | flops 58686464 | bytes 50606080 | tf_op jit(solution)/shard_map/vmap()/reduce_sum | solution.py:18
  159.1 0.1 multiply_reduce_fusion
  159.2 0.1 copy.12
  159.3 0.1 copy.16
  159.4 0.3 copy.14
  159.7 13.5 %all-gather.6.cloned.1.call-done = bf16[8192,1,128]{2,0,1:T(8,128)(2,1)} async-done(((bf16[256,1,128]{2,0,1:T(8,128)(2,1)}), bf16[8192,1,128]{2,0,1:T(8,128)(2,1)}) %all-gather.6.cloned.1.call-update) | async-done | bytes 2097168 | tf_op jit(solution)/shard_map/all_gather | solution.py:55
  173.2 0.0 copy-start.3
  173.2 17.4 %fusion.2 = f32[128,64,16]{0,2,1:T(8,128)S(1)} fusion(f32[32,64,16]{2,1,0:T(8,128)S(1)} %copy.14, bf16[32,256,128,1]{2,1,3,0:T(8,128)(2,1)} %bitcast.110, bf16[32,64,16,256]{3,1,2,0:T(8,128)(2,1)} %get-tuple-element.10), kind=kOutput, calls=%fused_computation.8 | convolution fusion | flops 2155741184 | bytes 19529728 | tf_op jit(solution)/shard_map/vmap(nkgc,ckd->nkgd)/dot_general | solution.py:19
  190.6 0.0 copy-done.3
  190.6 0.4 fusion.11
  191.1 0.0 copy-start.2
  191.1 0.8 copy.38
  191.8 0.0 all-gather.8.cloned.1.call-update
  191.9 0.0 reduce-scatter.2.cloned.1.call-start
  191.9 98.1 %all-gather.8.cloned.1.call-done = bf16[2048,2048]{1,0:T(8,128)(2,1)} async-done(((bf16[64,2048]{1,0:T(8,128)(2,1)}), bf16[2048,2048]{1,0:T(8,128)(2,1)}) %all-gather.8.cloned.1.call-update) | async-done | bytes 8388624 | tf_op jit(solution)/shard_map/all_gather | solution.py:71
  290.0 0.0 copy-done
  290.0 9.2 %convolution_convert_fusion = bf16[2048,512]{1,0:T(8,128)(2,1)} fusion(bf16[2048,2048]{1,0:T(8,128)(2,1)} %all-gather.8.cloned.1.call-done, bf16[2048,512]{1,0:T(8,128)(2,1)S(1)} %copy-done), kind=kOutput, calls=%fused_computation.17 | convolution fusion | flops 4296015872 | bytes 12582912 | tf_op jit(solution)/shard_map/dot_general | solution.py:70
  299.2 0.0 copy-done.2
  299.2 0.0 reduce-scatter.2.cloned.1.call-update
  299.2 50.0 %reduce-scatter.2.cloned.1.call-done = bf16[256,512]{1,0:T(8,128)(2,1)} async-done(((bf16[2048,512]{1,0:T(8,128)(2,1)}), bf16[256,512]{1,0:T(8,128)(2,1)}) %reduce-scatter.2.cloned.1.call-update) | async-done | bytes 262160 | tf_op jit(solution)/shard_map/reduce_scatter | solution.py:75
  (5 shorter events, 0.0 us)
Async XLA Ops:
  7.2 282.9 %copy-start = (bf16[2048,512]{1,0:T(8,128)(2,1)S(1)}, bf16[2048,512]{1,0:T(8,128)(2,1)}, u32[]{:S(2)}) copy-start(bf16[2048,512]{1,0:T(8,128)(2,1)} %param.15) | copy-start | bytes 6291460
  7.2 114.4 %all-gather.4.cloned.1.call-start = ((), (), s32[]{:S(2)}) async-start(), calls=%async_computation.1 | async-start | bytes 2162688 | tf_op jit(solution)/shard_map/all_gather | solution.py:54
  7.9 165.3 %all-gather.6.cloned.1.call-start = ((), (), s32[]{:S(2)}) async-start(), calls=%async_computation.2 | async-start | bytes 2162688 | tf_op jit(solution)/shard_map/all_gather | solution.py:55
  8.7 281.4 %all-gather.8.cloned.1.call-start = ((), (), s32[]{:S(2)}) async-start(), calls=%async_computation.3 | async-start | bytes 8650752 | tf_op jit(solution)/shard_map/all_gather | solution.py:71
  118.8 2.8 copy-start.1
  173.2 17.4 %copy-start.3 = (f32[64,16,128]{2,0,1:T(8,128)S(1)}, f32[64,16,128]{2,0,1:T(8,128)}, u32[]{:S(2)}) copy-start(f32[64,16,128]{2,0,1:T(8,128)} %fusion.6) | copy-start | bytes 1572868
  191.1 108.2 %copy-start.2 = (bf16[64,1,16,128]{3,2,0,1:T(8,128)(2,1)}, bf16[64,1,16,128]{3,2,0,1:T(8,128)(2,1)S(1)}, u32[]{:S(2)}) copy-start(bf16[64,1,16,128]{3,2,0,1:T(8,128)(2,1)S(1)} %fusion.11) | copy-start | bytes 786436
  191.9 157.3 %reduce-scatter.2.cloned.1.call-start = ((), (), s32[]{:S(2)}) async-start(), calls=%async_computation.4 | async-start | bytes 2359296 | tf_op jit(solution)/shard_map/reduce_scatter | solution.py:75
Sparse Core Ops, SparseCore 0:
  10.8 83.1 all-gather.3
  96.8 76.3 all-gather.5
  192.0 98.0 all-gather.7
  299.4 49.7 reduce-scatter.1
where the time goes:
time: 357 us; the launch traced here: 356 us
  waiting for transfers between devices  163 us (46%)
  blocking collectives  100 us (28%)
  matrix products  46.6 us (13%)
  other arithmetic  26.6 us (7%)
  between operations  15.2 us (4%)
  local copies, waits for them, and re-layouts  4.2 us (1%)
    all_gather x1, waiting for transfers between devices, per_device(): lax.all_gather(flattened, 'blk', axis=0, tiled=True)  98.1 us
    reduce_scatter x1, waiting for transfers between devices, per_device(): lax.psum_scatter(projection_terms.astype(jnp.bfloat16), 'head', scatter_d...  50 us
    all_gather x1, blocking collectives, per_device(): lax.all_gather(new_keys, 'blk', axis=0, tiled=True)  46.6 us
    all_gather x1, blocking collectives, per_device(): lax.all_gather(new_values, 'blk', axis=0, tiled=True)  38.5 us
    reduce_sum x2, other arithmetic, block_partial(): denominator = jnp.sum(weights.astype(jnp.float32), axis=-1)  25.2 us
    dot_general x2, matrix products, block_partial(): jnp.einsum('nkgc,ckd->nkgd', weights, value_block, preferred_element_type...  20.1 us
    dot_general x2, matrix products, block_partial(): jnp.einsum('nkgd,ckd->nkgc', query_block, key_block, preferred_element_ty...  17.4 us
    unnamed x1, blocking collectives  14.9 us
  transfers between devices with their start and end apart: 4, of which 3 were waited for; matrix products, arithmetic and copies ran while one was open for 14% of the time, Pallas kernels for 0%

commit v1 on v0

v1 whole, which is shorter than its diff:
```python
import functools
import math

import jax
import jax.numpy as jnp
from jax import lax
from jax.experimental import pallas as pl
from jax.experimental.pallas import tpu as pltpu
from jax.sharding import PartitionSpec as P

MESH = pl.DeviceIdType.MESH
F32 = jnp.float32
BF16 = jnp.bfloat16

QD = 64
CD = 256
HEADS = 16
HD = 128
ROWS = QD * HEADS
NZ = 8
KN0, VN0, META0, PKT = 2 * CD, 2 * CD + QD, 2 * CD + 2 * QD, 2 * CD + 2 * QD + 16
PAIRS = HEADS // 2
LOW = -1e30
SCALE = math.log2(math.e) / math.sqrt(HD)

KP = CD
KQ_MID = 448
AP = 4
AQ_MID = 6

RCHUNK = 128


def kernel(
    q_hbm, kn_hbm, vn_hbm, seg_ref, kc_hbm, vc_hbm, len_ref, w_hbm,
    att_hbm, out_hbm,
    kv, q_buf, segq, m_buf, acc, w_buf, abuf, att_f32, att_bf, psend, rx, keep, ysend, ry, out_buf,
    in_sem, w_sem, out_sem,
    kz_s, kz_r, ky_s, ky_r, kb_s, kb_r,
    az_s, az_r, ay_s, ay_r,
    x_s, x_r, f_s, f_r, wx_s, wx_r,
):
    b = lax.axis_index("blk")
    h = lax.axis_index("head")
    yh, z, c = b // 16, (b // 2) % NZ, b % 2
    x, yl = h // 2, h % 2
    oy, oc = 1 - yh, 1 - c

    def dev(yh_, z_, c_, x_, yl_):
        return {"blk": yh_ * 16 + z_ * 2 + c_, "head": x_ * 2 + yl_}

    right = dev(yh, (z + 1) % NZ, c, x, yl)
    left = dev(yh, (z + NZ - 1) % NZ, c, x, yl)
    across = dev(oy, z, c, x, yl)
    sibling = dev(yh, z, oc, x, yl)
    beside = dev(yh, z, c, x, 1 - yl)
    ring = (right, left)

    def rdma(src, dst, ss, rs, to):
        return pltpu.make_async_remote_copy(
            src_ref=src, dst_ref=dst, send_sem=ss, recv_sem=rs, device_id=to, device_id_type=MESH
        )

    mine = kv.at[c, yh, z]
    loads = [
        pltpu.make_async_copy(kc_hbm, mine.at[pl.ds(0, CD)], in_sem.at[0]),
        pltpu.make_async_copy(vc_hbm, mine.at[pl.ds(CD, CD)], in_sem.at[1]),
        pltpu.make_async_copy(kn_hbm, mine.at[pl.ds(KN0, QD)], in_sem.at[2]),
        pltpu.make_async_copy(vn_hbm, mine.at[pl.ds(VN0, QD)], in_sem.at[3]),
        pltpu.make_async_copy(q_hbm, q_buf, in_sem.at[4]),
    ]
    for cp in loads:
        cp.start()

    barrier = pltpu.get_barrier_semaphore()
    partners = [right, left, across, sibling, beside]
    for dx in (1, 2, 3):
        for cc in (0, 1):
            partners.append(dev(yh, z, cc, (x + dx) % 4, yl))
    for to in partners:
        pl.semaphore_signal(barrier, inc=1, device_id=to, device_id_type=MESH)

    length = len_ref[0]
    seg_row = seg_ref[...].astype(F32)
    for cp in loads[:4]:
        cp.wait()
    shown = lax.broadcasted_iota(jnp.int32, (CD, HD), 0) < length
    keys = kv[c, yh, z, 0:CD, :].astype(F32)
    kv[c, yh, z, 0:CD, :] = jnp.where(shown, keys, keys[0:1, :]).astype(BF16)
    values = kv[c, yh, z, CD : 2 * CD, :].astype(F32)
    kv[c, yh, z, CD : 2 * CD, :] = jnp.where(shown, values, 0.0).astype(BF16)
    top = lax.broadcasted_iota(jnp.int32, (16, HD), 0) < 8
    kv[c, yh, z, META0:PKT, :] = jnp.where(
        top, jnp.broadcast_to(seg_row, (16, HD)), length.astype(F32)
    ).astype(BF16)

    pl.semaphore_wait(barrier, len(partners))

    class Gather:
        def __init__(self, slot, p, qs, qa, qb, zs, zr, ys, yr, sib=None):
            self.slot, self.p, self.q, self.qa, self.qb = slot, p, qs, qa, qb
            self.zs, self.zr, self.ys, self.yr, self.sib = zs, zr, ys, yr, sib
            self.sent = []

        def z_of(self, d, s):
            return (z + NZ - s) % NZ if d == 0 else (z + s) % NZ

        def part(self, kind, d, s):
            if kind < 2:
                if s == 4 and kind != d:
                    return None
                return self.p
            if s == 4:
                return self.qa if d == 0 else self.qb
            return self.q

        def view(self, kind, d, s):
            zo = self.z_of(d, s)
            pc = self.part(kind, d, s)
            return self.slot(oy if kind == 1 else yh, zo, pc)

        def z_send(self, kind, d, s):
            if self.part(kind, d, s) is None:
                return
            zo = self.z_of(d, s - 1)
            ref = self.slot(oy if kind == 1 else yh, zo, self.part(kind, d, s))
            cp = rdma(ref, ref, self.zs.at[d, s - 1, kind], self.zr.at[d, s - 1, kind], ring[d])
            cp.start()
            self.sent.append(cp)

        def z_wait(self, kind, d, s):
            if self.part(kind, d, s) is None:
                return
            ref = self.view(kind, d, s)
            rdma(ref, ref, self.zs.at[d, s - 1, kind], self.zr.at[d, s - 1, kind], ring[d]).wait_recv()

        def code(self, d, s):
            return 0 if s == 0 else (1 + d * 3 + s - 1 if s < 4 else 7 + d)

        def y_piece(self, d, s):
            return self.q if s < 4 else (self.qa if d == 0 else self.qb)

        def y_send(self, d, s):
            k = self.code(d, s)
            ref = self.slot(yh, self.z_of(d, s), self.y_piece(d, s))
            cp = rdma(ref, ref, self.ys.at[k], self.yr.at[k], across)
            cp.start()
            self.sent.append(cp)

        def y_wait(self, d, s):
            k = self.code(d, s)
            ref = self.slot(oy, self.z_of(d, s), self.y_piece(d, s))
            rdma(ref, ref, self.ys.at[k], self.yr.at[k], across).wait_recv()

        def yp_send(self):
            ref = self.slot(yh, z, self.p)
            cp = rdma(ref, ref, self.ys.at[9], self.yr.at[9], across)
            cp.start()
            self.sent.append(cp)

        def yp_wait(self):
            ref = self.slot(oy, z, self.p)
            rdma(ref, ref, self.ys.at[9], self.yr.at[9], across).wait_recv()

        def b_ref(self, kind, d, s, core):
            pc = self.p if kind < 2 else self.y_piece(d, s)
            return kv.at[core, oy if kind % 2 else yh, self.z_of(d, s), pl.ds(pc[0], pc[1])]

        def b_send(self, kind, d, s):
            if self.sib is None:
                return
            if kind < 2 and s > 0 and self.part(kind, d, s) is None:
                return
            k = self.code(d, s)
            ref = self.b_ref(kind, d, s, c)
            cp = rdma(ref, ref, self.sib[0].at[kind, k], self.sib[1].at[kind, k], sibling)
            cp.start()
            self.sent.append(cp)

        def b_wait(self, d, s):
            for kind in range(4):
                if kind < 2 and s > 0 and self.part(kind, d, s) is None:
                    continue
                k = self.code(d, s)
                ref = self.b_ref(kind, d, s, oc)
                rdma(ref, ref, self.sib[0].at[kind, k], self.sib[1].at[kind, k], sibling).wait_recv()

        def open(self):
            self.yp_send()
            for d in (0, 1):
                self.z_send(0, d, 1)
            self.y_send(0, 0)
            for d in (0, 1):
                self.z_send(2, d, 1)
            self.b_send(0, 0, 0)
            self.b_send(2, 0, 0)

        def middle(self):
            self.yp_wait()
            for d in (0, 1):
                self.z_send(1, d, 1)
            self.b_send(1, 0, 0)

        def step(self, s):
            for kind in (0, 2, 1):
                for d in (0, 1):
                    if self.part(kind, d, s) is None:
                        continue
                    self.z_wait(kind, d, s)
                    if s < 4:
                        self.z_send(kind, d, s + 1)
                    if kind == 2:
                        self.y_send(d, s)
                    self.b_send(kind, d, s)

        def late(self, s):
            for d in (0, 1) if s > 0 else (0,):
                self.y_wait(d, s)
                self.b_send(3, d, s)

        def finish(self):
            for cp in self.sent:
                cp.wait_send()

    def kv_slot(y_, z_, pc):
        return kv.at[c, y_, z_, pl.ds(pc[0], pc[1])]

    gk = Gather(
        kv_slot, (0, KP), (KP, PKT - KP), (KP, KQ_MID - KP), (KQ_MID, PKT - KQ_MID),
        kz_s, kz_r, ky_s, ky_r, (kb_s, kb_r),
    )
    gk.open()

    wl, wx = [], []
    for i in (0, 1):
        half = w_hbm.at[:, pl.ds(i * 256, 256)]
        cp = pltpu.make_async_copy(half, w_buf.at[2 * c + i], w_sem.at[i])
        cp.start()
        wl.append(cp)
        cp = rdma(half, w_buf.at[2 * c + i], wx_s.at[i], wx_r.at[i], sibling)
        cp.start()
        wx.append(cp)

    cols = jnp.broadcast_to(seg_row, (HD, HD)).T[0:QD, :]
    segq[...] = jnp.broadcast_to(cols[:, None, :], (QD, HEADS, HD)).reshape(ROWS, HD)
    m_buf[...] = jnp.full((ROWS, HD), LOW, F32)
    acc[...] = jnp.zeros((ROWS, 2 * HD), F32)
    loads[4].wait()

    lane = lax.broadcasted_iota(jnp.int32, (1, CD), 1)
    lane_blk = (lane // 128) * 16 + (lane // 64) % 2

    def attend(zo, first):
        order = [(0, 0), (0, 1), (1, 0), (1, 1)]
        key_blk = lane_blk + zo * 2
        seg0 = [kv[c_, y_, zo, META0:PKT, :][0:1, :].astype(F32) for y_, c_ in order]
        lens = [kv[c_, y_, zo, META0:PKT, :][8:9, :].astype(F32) for y_, c_ in order]
        low = lax.broadcasted_iota(jnp.int32, (1, HD), 1) < QD
        seg_k = jnp.concatenate([jnp.where(low, seg0[0], seg0[1]), jnp.where(low, seg0[2], seg0[3])], axis=1)
        seg_k = jnp.where(key_blk <= b, seg_k, -1.0)
        slot = lax.broadcasted_iota(jnp.int32, (CD, HD), 0).astype(F32)
        counts = [jnp.where(slot < ln, 1.0, 0.0).astype(BF16) for ln in lens]

        def body(r, carry):
            rows = pl.ds(pl.multiple_of(r * RCHUNK, RCHUNK), RCHUNK)
            q = q_buf[rows, :]
            scores = [
                lax.dot_general(
                    q, kv[c_, y_, zo, 0:CD, :], (((1,), (1,)), ((), ())), preferred_element_type=F32
                )
                for y_, c_ in order
            ]
            fresh = jnp.concatenate([kv[c_, y_, zo, KN0 : KN0 + QD, :] for y_, c_ in order], axis=0)
            s_new = lax.dot_general(q, fresh, (((1,), (1,)), ((), ())), preferred_element_type=F32)
            sq = segq[rows, :]
            sees = jnp.concatenate([sq, sq], axis=1) == seg_k
            if first:
                tok = (lax.broadcasted_iota(jnp.int32, (RCHUNK, CD), 0) + r * RCHUNK) // HEADS
                sees = sees & (key_blk * QD + lane % QD <= tok + b * QD)
            s_new = jnp.where(sees, s_new, LOW)
            scores.append(s_new)
            tops = functools.reduce(jnp.maximum, scores)
            tops = jnp.max(tops, axis=1, keepdims=True)
            m_old = m_buf[rows, :]
            m_new = jnp.maximum(m_old, tops)
            m_buf[rows, :] = m_new
            shrink = jnp.exp2((m_old - m_new) * SCALE)
            base = m_new * SCALE
            base2 = jnp.concatenate([base, base], axis=1)
            total = acc[rows, :] * jnp.concatenate([shrink, shrink], axis=1)
            for i, s in enumerate(scores):
                w = jnp.exp2(s * SCALE - base2).astype(BF16)
                if i < 4:
                    y_, c_ = order[i]
                    rhs = jnp.concatenate([kv[c_, y_, zo, CD : 2 * CD, :], counts[i]], axis=1)
                else:
                    fresh_v = jnp.concatenate(
                        [kv[c_, y_, zo, VN0 : VN0 + QD, :] for y_, c_ in order], axis=0
                    )
                    rhs = jnp.concatenate([fresh_v, jnp.ones((CD, HD), BF16)], axis=1)
                total = total + jnp.dot(w, rhs, preferred_element_type=F32)
            acc[rows, :] = total
            return carry

        lax.fori_loop(0, ROWS // RCHUNK, body, 0)

    gk.middle()
    gk.late(0)
    gk.b_wait(0, 0)
    attend(z, True)
    for s in (1, 2, 3, 4):
        gk.step(s)
        if s > 1:
            for d in (0, 1):
                gk.b_wait(d, s - 1)
                attend(gk.z_of(d, s - 1), False)
        gk.late(s)
    for d in (0, 1):
        gk.b_wait(d, 4)
    attend(gk.z_of(0, 4), False)

    def finish_rows(r, carry):
        rows = pl.ds(pl.multiple_of(r * RCHUNK, RCHUNK), RCHUNK)
        o = acc[rows, 0:HD] / acc[rows, HD : 2 * HD]
        att_f32[rows, :] = o
        att_bf[rows, :] = o.astype(BF16)
        return carry

    lax.fori_loop(0, ROWS // RCHUNK, finish_rows, 0)
    for i in range(HEADS):
        abuf[yh, z, i // 2, :, (i % 2) * HD : (i % 2 + 1) * HD] = att_f32[
            pl.ds(i, QD, stride=HEADS), :
        ].astype(BF16)

    ga = Gather(
        lambda y_, z_, pc: abuf.at[y_, z_, pl.ds(pc[0], pc[1])],
        (0, AP), (AP, PAIRS - AP), (AP, AQ_MID - AP), (AQ_MID, PAIRS - AQ_MID),
        az_s, az_r, ay_s, ay_r,
    )
    ga.open()
    att_out = pltpu.make_async_copy(att_bf, att_hbm, out_sem.at[0])
    att_out.start()
    for cp in wl:
        cp.wait()
    for cp in wx:
        cp.wait()

    x_items = []

    def project(items):
        n_rows = len(items) * QD

        def body(n, carry):
            total = jnp.zeros((n_rows, 256), F32)
            for j in range(PAIRS):
                lhs = jnp.concatenate([abuf[y_, z_, j] for y_, z_ in items], axis=0)
                total = total + jnp.dot(
                    lhs, w_buf[n, j * 256 : (j + 1) * 256, :], preferred_element_type=F32
                )
            for i, (y_, z_) in enumerate(items):
                psend[y_, z_, n] = total[i * QD : (i + 1) * QD].astype(BF16)
            return carry

        lax.fori_loop(0, 4, body, 0)
        for y_, z_ in items:
            owner = 2 * y_ + z_ // 4
            for cc in (0, 1):
                to_c = c if cc == 0 else oc
                src = psend.at[y_, z_, pl.ds(2 * to_c, 2)]
                dst = rx.at[x, c, z_ % 4]
                ss = x_s.at[y_, z_, cc]
                rs = x_r.at[x, c, z_ % 4]
                cp = rdma(src, dst, ss, rs, dev(yh, z, to_c, owner, yl))
                if cc == 1:
                    cp.start()
                else:
                    here = pltpu.make_async_copy(src, dst, rs)

                    @pl.when(owner == x)
                    def _():
                        here.start()

                    @pl.when(owner != x)
                    def _():
                        cp.start()

                x_items.append((cp, owner, cc))

    ga.middle()
    ga.late(0)
    project([(yh, z), (oy, z)])
    for s in (1, 2, 3, 4):
        ga.step(s)
        if s > 1:
            zr, zl = ga.z_of(0, s - 1), ga.z_of(1, s - 1)
            project([(yh, zr), (oy, zr), (yh, zl), (oy, zl)])
        ga.late(s)
    zr = ga.z_of(0, 4)
    project([(yh, zr), (oy, zr)])

    def x_wait(cc, zq):
        for xs in range(4):
            ref = rx.at[xs, cc, zq]
            pltpu.make_async_copy(ref, ref, x_r.at[xs, cc, zq]).wait()

    def x_sum(cc, zq, half):
        total = rx[0, cc, zq, half].astype(F32)
        for xs in range(1, 4):
            total = total + rx[xs, cc, zq, half].astype(F32)
        return total

    sends = []
    for e in (0, 1):
        for cc in (0, 1):
            zq = 2 * (1 - yl) + e
            x_wait(cc, zq)
            for half in (0, 1):
                ysend[e, cc, half] = x_sum(cc, zq, half).astype(BF16)
            cp = rdma(ysend.at[e, cc], ry.at[e, cc], f_s.at[e, cc], f_r.at[e, cc], beside)
            cp.start()
            sends.append(cp)
    for e in (0, 1):
        for cc in (0, 1):
            zq = 2 * yl + e
            x_wait(cc, zq)
            for half in (0, 1):
                keep[e, cc, half] = x_sum(cc, zq, half)
    k = 0
    for e in (0, 1):
        for cc in (0, 1):
            sends[k].wait_recv()
            k += 1
            for half in (0, 1):
                out_buf[(e * 2 + cc) * QD : (e * 2 + cc + 1) * QD, half * 256 : (half + 1) * 256] = (
                    keep[e, cc, half] + ry[e, cc, half].astype(F32)
                ).astype(BF16)
    proj_out = pltpu.make_async_copy(out_buf, out_hbm, out_sem.at[1])
    proj_out.start()

    for cp in sends:
        cp.wait_send()
    for cp, owner, cc in x_items:
        if cc == 1:
            cp.wait_send()
        else:

            @pl.when(owner != x)
            def _():
                cp.wait_send()

    gk.finish()
    ga.finish()
    att_out.wait()
    proj_out.wait()


def per_device(queries, new_keys, new_values, segment_ids, cache_keys, cache_values, cache_lengths, o_weight):
    any_ = pl.BlockSpec(memory_space=pl.ANY)
    vmem = pl.BlockSpec(memory_space=pltpu.VMEM)
    smem = pl.BlockSpec(memory_space=pltpu.SMEM)
    dma = pltpu.SemaphoreType.DMA
    seg2 = jnp.concatenate([segment_ids, segment_ids]).reshape(1, 2 * QD)
    att, out = pl.pallas_call(
        kernel,
        out_shape=(
            jax.ShapeDtypeStruct((ROWS, HD), BF16),
            jax.ShapeDtypeStruct((4 * QD, 512), BF16),
        ),
        in_specs=[any_, any_, any_, vmem, any_, any_, smem, any_],
        out_specs=(any_, any_),
        scratch_shapes=[
            pltpu.VMEM((2, 2, NZ, PKT, HD), BF16),
            pltpu.VMEM((ROWS, HD), BF16),
            pltpu.VMEM((ROWS, HD), F32),
            pltpu.VMEM((ROWS, HD), F32),
            pltpu.VMEM((ROWS, 2 * HD), F32),
            pltpu.VMEM((4, HEADS * HD, 256), BF16),
            pltpu.VMEM((2, NZ, PAIRS, QD, 256), BF16),
            pltpu.VMEM((ROWS, HD), F32),
            pltpu.VMEM((ROWS, HD), BF16),
            pltpu.VMEM((2, NZ, 4, QD, 256), BF16),
            pltpu.VMEM((4, 2, 4, 2, QD, 256), BF16),
            pltpu.VMEM((2, 2, 2, QD, 256), F32),
            pltpu.VMEM((2, 2, 2, QD, 256), BF16),
            pltpu.VMEM((2, 2, 2, QD, 256), BF16),
            pltpu.VMEM((4 * QD, 512), BF16),
            dma((5,)), dma((2,)), dma((2,)),
            dma((2, 4, 3)), dma((2, 4, 3)), dma((10,)), dma((10,)), dma((4, 9)), dma((4, 9)),
            dma((2, 4, 3)), dma((2, 4, 3)), dma((10,)), dma((10,)),
            dma((2, NZ, 2)), dma((4, 2, 4)), dma((2, 2)), dma((2, 2)), dma((2,)), dma((2,)),
        ],
        compiler_params=pltpu.CompilerParams(
            collective_id=0, has_side_effects=True, vmem_limit_bytes=56 << 20
        ),
    )(
        queries.reshape(ROWS, HD),
        new_keys.reshape(QD, HD),
        new_values.reshape(QD, HD),
        seg2,
        cache_keys.reshape(CD, HD),
        cache_values.reshape(CD, HD),
        cache_lengths,
        o_weight,
    )
    return att.reshape(QD, HEADS, HD), out


def solution(mesh):
    return jax.shard_map(
        per_device,
        mesh=mesh,
        in_specs=(
            P("blk", "head", None),
            P("blk", "head", None),
            P("blk", "head", None),
            P("blk"),
            P("blk", "head", None),
            P("blk", "head", None),
            P("blk"),
            P("head", "blk"),
        ),
        out_specs=(P("blk", "head", None), P("head", "blk")),
        check_vma=False,
    )
```

time: 357 us -> 140 us (0.39)
  the two profiles are of different devices: /device:TPU:2 before, /device:TPU:95 now
where the time goes in v1:
time: 140 us
  Pallas kernels  134 us (96%)
  local copies, waits for them, and re-layouts  3.34 us (2%)
    pallas_call x1, Pallas kernels, per_device(): pl.pallas_call(kernel, out_shape=(jax.ShapeDtypeStruct((ROWS, HD), BF16),...  134 us
    unnamed x2, local copies, waits for them, and re-layouts  3.34 us

profile of v1, /device:TPU:95, one launch (start us, length us, event | category | flops | bytes accessed | tf_op | source)
XLA Modules:
  0.0 139.6 jit_solution(8571358218333840417)
XLA Ops:
  1.3 1.3 add_bitcast_fusion.seg_ref
  2.6 133.7 %shard_map.95 = (bf16[1024,128]{1,0:T(8,128)(2,1)}, bf16[256,512]{1,0:T(8,128)(2,1)}) custom-call(bf16[1024,128]{1,0:T(8,128)(2,1)} %bitcast.8, bf16[64,128]{1,0:T(8,128)(2,1)} %bitcast.12, bf16[64,128]{1,0:T(8,128)(2,1)} %bitcast.13, s32[1,128]{1,0:T(1,128)} %add_bitcast_fusion.seg_ref, bf16[256,128]{1,0:T(8,128)(2,1)} %bitcast.10, ...), custom_call_target="tpu_custom_call" | custom-call | tf_op jit(solution)/shard_map/pallas_call | solution.py:463
  136.3 1.7 %copy.13 = bf16[64,16,128]{2,1,0:T(8,128)(2,1)} copy(bf16[64,16,128]{2,1,0:T(8,128)(2,1)} %bitcast.9) | data formatting | bytes 524288
  138.0 1.7 %copy.14 = bf16[256,512]{1,0:T(8,128)(2,1)} copy(bf16[256,512]{1,0:T(8,128)(2,1)} %get-tuple-element.9) | data formatting | bytes 524288

commit v2 on v1

v2 whole, which is shorter than its diff:
```python
import functools
import math

import jax
import jax.numpy as jnp
from jax import lax
from jax.experimental import pallas as pl
from jax.experimental.pallas import tpu as pltpu
from jax.sharding import PartitionSpec as P

MESH = pl.DeviceIdType.MESH
F32 = jnp.float32
BF16 = jnp.bfloat16

QD = 64
CD = 256
HEADS = 16
HD = 128
ROWS = QD * HEADS
NZ = 8
KN0, VN0, META0, PKT = 2 * CD, 2 * CD + QD, 2 * CD + 2 * QD, 2 * CD + 2 * QD + 16
PAIRS = HEADS // 2
LOW = -1e30
SCALE = math.log2(math.e) / math.sqrt(HD)

KP = 448
KQ_MID = 560
AP = 5
AQ_MID = 6

RCHUNK = 256


def kernel(
    q_hbm, kn_hbm, vn_hbm, seg_ref, kc_hbm, vc_hbm, len_ref, w_hbm,
    att_hbm, out_hbm,
    kv, q_buf, segq, m_buf, acc, sc, m_next, vb, w_buf, abuf, att_f32, att_bf, psend, rx, keep, ysend, ry, out_buf,
    in_sem, w_sem, out_sem,
    kz_s, kz_r, ky_s, ky_r, kb_s, kb_r,
    az_s, az_r, ay_s, ay_r,
    x_s, x_r, f_s, f_r, wx_s, wx_r,
):
    b = lax.axis_index("blk")
    h = lax.axis_index("head")
    yh, z, c = b // 16, (b // 2) % NZ, b % 2
    x, yl = h // 2, h % 2
    oy, oc = 1 - yh, 1 - c

    def dev(yh_, z_, c_, x_, yl_):
        return {"blk": yh_ * 16 + z_ * 2 + c_, "head": x_ * 2 + yl_}

    right = dev(yh, (z + 1) % NZ, c, x, yl)
    left = dev(yh, (z + NZ - 1) % NZ, c, x, yl)
    across = dev(oy, z, c, x, yl)
    sibling = dev(yh, z, oc, x, yl)
    beside = dev(yh, z, c, x, 1 - yl)
    ring = (right, left)

    def rdma(src, dst, ss, rs, to):
        return pltpu.make_async_remote_copy(
            src_ref=src, dst_ref=dst, send_sem=ss, recv_sem=rs, device_id=to, device_id_type=MESH
        )

    barrier = pltpu.get_barrier_semaphore()
    partners = [right, left, across, sibling, beside]
    for dx in (1, 2, 3):
        for cc in (0, 1):
            partners.append(dev(yh, z, cc, (x + dx) % 4, yl))
    for to in partners:
        pl.semaphore_signal(barrier, inc=1, device_id=to, device_id_type=MESH)

    mine = kv.at[c, yh, z]
    loads = [
        pltpu.make_async_copy(kc_hbm, mine.at[pl.ds(0, CD)], in_sem.at[0]),
        pltpu.make_async_copy(vc_hbm, mine.at[pl.ds(CD, CD)], in_sem.at[1]),
        pltpu.make_async_copy(kn_hbm, mine.at[pl.ds(KN0, QD)], in_sem.at[2]),
        pltpu.make_async_copy(vn_hbm, mine.at[pl.ds(VN0, QD)], in_sem.at[3]),
        pltpu.make_async_copy(q_hbm, q_buf, in_sem.at[4]),
    ]
    for cp in loads:
        cp.start()

    length = len_ref[0]
    seg_row = seg_ref[...].astype(F32)
    seg_row = jnp.concatenate([seg_row, seg_row], axis=1)
    for cp in loads[:4]:
        cp.wait()
    shown = lax.broadcasted_iota(jnp.int32, (CD, HD), 0) < length
    keys = kv[c, yh, z, 0:CD, :].astype(F32)
    kv[c, yh, z, 0:CD, :] = jnp.where(shown, keys, keys[0:1, :]).astype(BF16)
    values = kv[c, yh, z, CD : 2 * CD, :].astype(F32)
    kv[c, yh, z, CD : 2 * CD, :] = jnp.where(shown, values, 0.0).astype(BF16)
    top = lax.broadcasted_iota(jnp.int32, (16, HD), 0) < 8
    kv[c, yh, z, META0:PKT, :] = jnp.where(
        top, jnp.broadcast_to(seg_row, (16, HD)), length.astype(F32)
    ).astype(BF16)

    pl.semaphore_wait(barrier, len(partners))

    class Gather:
        def __init__(self, slot, p, qs, qa, qb, zs, zr, ys, yr, sib=None):
            self.slot, self.p, self.q, self.qa, self.qb = slot, p, qs, qa, qb
            self.zs, self.zr, self.ys, self.yr, self.sib = zs, zr, ys, yr, sib
            self.sent = []

        def go(self, copy):
            copy().start()
            self.sent.append(copy)

        def z_of(self, d, s):
            return (z + NZ - s) % NZ if d == 0 else (z + s) % NZ

        def part(self, kind, d, s):
            if kind < 2:
                if s == 4 and kind != d:
                    return None
                return self.p
            if s == 4:
                return self.qa if d == 0 else self.qb
            return self.q

        def view(self, kind, d, s):
            return self.slot(oy if kind == 1 else yh, self.z_of(d, s), self.part(kind, d, s))

        def z_send(self, kind, d, s):
            if self.part(kind, d, s) is None:
                return

            def copy():
                ref = self.slot(oy if kind == 1 else yh, self.z_of(d, s - 1), self.part(kind, d, s))
                return rdma(ref, ref, self.zs.at[d, s - 1, kind], self.zr.at[d, s - 1, kind], ring[d])

            self.go(copy)

        def z_wait(self, kind, d, s):
            if self.part(kind, d, s) is None:
                return
            ref = self.view(kind, d, s)
            rdma(ref, ref, self.zs.at[d, s - 1, kind], self.zr.at[d, s - 1, kind], ring[d]).wait_recv()

        def code(self, d, s):
            return 0 if s == 0 else (1 + d * 3 + s - 1 if s < 4 else 7 + d)

        def y_piece(self, d, s):
            return self.q if s < 4 else (self.qa if d == 0 else self.qb)

        def y_send(self, d, s):
            def copy():
                k = self.code(d, s)
                ref = self.slot(yh, self.z_of(d, s), self.y_piece(d, s))
                return rdma(ref, ref, self.ys.at[k], self.yr.at[k], across)

            self.go(copy)

        def y_wait(self, d, s):
            k = self.code(d, s)
            ref = self.slot(oy, self.z_of(d, s), self.y_piece(d, s))
            rdma(ref, ref, self.ys.at[k], self.yr.at[k], across).wait_recv()

        def yp_send(self):
            def copy():
                ref = self.slot(yh, z, self.p)
                return rdma(ref, ref, self.ys.at[9], self.yr.at[9], across)

            self.go(copy)

        def yp_wait(self):
            ref = self.slot(oy, z, self.p)
            rdma(ref, ref, self.ys.at[9], self.yr.at[9], across).wait_recv()

        def b_ref(self, kind, d, s, core):
            pc = self.p if kind < 2 else self.y_piece(d, s)
            return kv.at[core, oy if kind % 2 else yh, self.z_of(d, s), pl.ds(pc[0], pc[1])]

        def b_send(self, kind, d, s):
            if self.sib is None:
                return
            if kind < 2 and s > 0 and self.part(kind, d, s) is None:
                return

            def copy():
                k = self.code(d, s)
                ref = self.b_ref(kind, d, s, c)
                return rdma(ref, ref, self.sib[0].at[kind, k], self.sib[1].at[kind, k], sibling)

            self.go(copy)

        def b_wait(self, d, s):
            for kind in range(4):
                if kind < 2 and s > 0 and self.part(kind, d, s) is None:
                    continue
                k = self.code(d, s)
                ref = self.b_ref(kind, d, s, oc)
                rdma(ref, ref, self.sib[0].at[kind, k], self.sib[1].at[kind, k], sibling).wait_recv()

        def open(self):
            self.yp_send()
            for kind in (2, 0):
                for d in (0, 1):
                    self.z_send(kind, d, 1)
                if kind == 2:
                    self.y_send(0, 0)
                self.b_send(kind, 0, 0)

        def middle(self):
            self.yp_wait()
            for d in (0, 1):
                self.z_send(1, d, 1)
            self.b_send(1, 0, 0)

        def forward(self, kinds, s):
            for kind in kinds:
                for d in (0, 1):
                    if self.part(kind, d, s) is None:
                        continue
                    self.z_wait(kind, d, s)
                    if s < 4:
                        self.z_send(kind, d, s + 1)
                    if kind == 2:
                        self.y_send(d, s)
                    self.b_send(kind, d, s)

        def late(self, s):
            for d in (0, 1) if s > 0 else (0,):
                self.y_wait(d, s)
                self.b_send(3, d, s)

        def finish(self):
            for copy in self.sent:
                copy().wait_send()

    def kv_slot(y_, z_, pc):
        return kv.at[c, y_, z_, pl.ds(pc[0], pc[1])]

    gk = Gather(
        kv_slot, (0, KP), (KP, PKT - KP), (KP, KQ_MID - KP), (KQ_MID, PKT - KQ_MID),
        kz_s, kz_r, ky_s, ky_r, (kb_s, kb_r),
    )
    gk.open()

    cols = jnp.broadcast_to(seg_row, (HD, HD)).T[0:QD, :]
    segq[...] = jnp.broadcast_to(cols[:, None, :], (QD, HEADS, HD)).reshape(ROWS, HD)
    m_buf[...] = jnp.full((ROWS, HD), LOW, F32)
    acc[...] = jnp.zeros((ROWS, 2 * HD), F32)
    loads[4].wait()

    lane = lax.broadcasted_iota(jnp.int32, (1, CD), 1)
    lane_blk = (lane // 128) * 16 + (lane // 64) % 2
    order = [(0, 0), (0, 1), (1, 0), (1, 1)]

    def attend(zo):
        key_blk = lane_blk + zo * 2
        seg0 = [kv[c_, y_, zo, META0:PKT, :][0:1, :].astype(F32) for y_, c_ in order]
        lens = [kv[c_, y_, zo, META0:PKT, :][8:9, :].astype(F32) for y_, c_ in order]
        low = lax.broadcasted_iota(jnp.int32, (1, HD), 1) < QD
        seg_k = jnp.concatenate([jnp.where(low, seg0[0], seg0[1]), jnp.where(low, seg0[2], seg0[3])], axis=1)
        key_row = key_blk * QD + lane % QD
        slot = lax.broadcasted_iota(jnp.int32, (CD, HD), 0).astype(F32)
        for i, (y_, c_) in enumerate(order):
            vb[i * CD : (i + 1) * CD, 0:HD] = kv[c_, y_, zo, CD : 2 * CD, :]
            vb[i * CD : (i + 1) * CD, HD : 2 * HD] = jnp.where(slot < lens[i], 1.0, 0.0).astype(BF16)
            vb[4 * CD + i * QD : 4 * CD + (i + 1) * QD, 0:HD] = kv[c_, y_, zo, VN0 : VN0 + QD, :]
        vb[4 * CD : 5 * CD, HD : 2 * HD] = jnp.ones((CD, HD), BF16)

        def scores(r):
            rows = pl.ds(r * RCHUNK, RCHUNK)
            q = q_buf[rows, :]
            tops = None
            for i in range(5):
                if i < 4:
                    y_, c_ = order[i]
                    keys = kv[c_, y_, zo, 0:CD, :]
                else:
                    keys = jnp.concatenate([kv[c_, y_, zo, KN0 : KN0 + QD, :] for y_, c_ in order], axis=0)
                s = lax.dot_general(q, keys, (((1,), (1,)), ((), ())), preferred_element_type=F32)
                if i == 4:
                    sq = segq[rows, :]
                    sees = jnp.concatenate([sq, sq], axis=1) == seg_k
                    tok = (lax.broadcasted_iota(jnp.int32, (RCHUNK, CD), 0) + r * RCHUNK) // HEADS
                    s = jnp.where(sees & (key_row <= tok + b * QD), s, LOW)
                sc[r % 2, :, i * CD : (i + 1) * CD] = s
                top = jnp.maximum(s[:, 0:HD], s[:, HD : 2 * HD])
                tops = top if tops is None else jnp.maximum(tops, top)
            m_next[r % 2] = jnp.maximum(m_buf[rows, :], jnp.max(tops, axis=1, keepdims=True))

        def weigh(r):
            rows = pl.ds(r * RCHUNK, RCHUNK)
            m_new = m_next[r % 2]
            shrink = jnp.exp2((m_buf[rows, :] - m_new) * SCALE)
            m_buf[rows, :] = m_new
            base = m_new * SCALE
            w = jnp.concatenate(
                [
                    jnp.exp2(sc[r % 2, :, i * HD : (i + 1) * HD] * SCALE - base).astype(BF16)
                    for i in range(10)
                ],
                axis=1,
            )
            acc[rows, :] = acc[rows, :] * jnp.concatenate([shrink, shrink], axis=1) + jnp.dot(
                w, vb[...], preferred_element_type=F32
            )

        n = ROWS // RCHUNK
        scores(0)
        for r in range(n):
            if r + 1 < n:
                scores(r + 1)
            weigh(r)

    def group_z(k):
        s = (k + 1) // 2
        return (z + (1 - 2 * (k % 2)) * s + NZ) % NZ

    def before(g, k, wait):
        if k == 0:
            g.middle()
            g.late(0)
            g.forward((2,), 1)
            if wait:
                g.b_wait(0, 0)
            return
        s = (k + 1) // 2
        if k % 2:
            g.forward((0, 1), s)
            g.late(s)
            if wait:
                g.b_wait(0, s)
                if s == 4:
                    g.b_wait(1, s)
        else:
            g.forward((2,), s + 1)
            if wait:
                g.b_wait(1, s)

    def weights(i):
        half = w_hbm.at[:, pl.ds(i * 256, 256)]
        slot = w_buf.at[2 * c + i]
        here = pltpu.make_async_copy(half, slot, w_sem.at[i])
        return here, rdma(half, slot, wx_s.at[i], wx_r.at[i], sibling)

    def kv_group(k, carry):
        for i in range(8):

            @pl.when(k == i)
            def _():
                before(gk, i, True)
                if i in (2, 3):
                    for cp in weights(i - 2):
                        cp.start()

        attend(group_z(k))
        return carry

    lax.fori_loop(0, 8, kv_group, 0)

    def finish_rows(r, carry):
        rows = pl.ds(pl.multiple_of(r * RCHUNK, RCHUNK), RCHUNK)
        o = acc[rows, 0:HD] / acc[rows, HD : 2 * HD]
        att_f32[rows, :] = o
        att_bf[rows, :] = o.astype(BF16)
        return carry

    lax.fori_loop(0, ROWS // RCHUNK, finish_rows, 0)
    for i in range(HEADS):
        abuf[yh, z, i // 2, :, (i % 2) * HD : (i % 2 + 1) * HD] = att_f32[
            pl.ds(i, QD, stride=HEADS), :
        ].astype(BF16)

    ga = Gather(
        lambda y_, z_, pc: abuf.at[y_, z_, pl.ds(pc[0], pc[1])],
        (0, AP), (AP, PAIRS - AP), (AP, AQ_MID - AP), (AQ_MID, PAIRS - AQ_MID),
        az_s, az_r, ay_s, ay_r,
    )
    ga.open()
    att_out = pltpu.make_async_copy(att_bf, att_hbm, out_sem.at[0])
    att_out.start()
    for i in (0, 1):
        for cp in weights(i):
            cp.wait()

    def x_copy(y_, z_, cc):
        to_c = c if cc == 0 else oc
        owner = 2 * y_ + z_ // 4
        src = psend.at[y_, z_, pl.ds(2 * to_c, 2)]
        dst = rx.at[x, c, z_ % 4]
        rs = x_r.at[x, c, z_ % 4]
        away = rdma(src, dst, x_s.at[y_, z_, cc], rs, dev(yh, z, to_c, owner, yl))
        return away, (src, dst, rs), owner

    def project(zo):
        def body(n, carry):
            total = jnp.zeros((2 * QD, 256), F32)
            for j in range(PAIRS):
                lhs = jnp.concatenate([abuf[yh, zo, j], abuf[oy, zo, j]], axis=0)
                total = total + jnp.dot(
                    lhs, w_buf[n, j * 256 : (j + 1) * 256, :], preferred_element_type=F32
                )
            psend[yh, zo, n] = total[0:QD].astype(BF16)
            psend[oy, zo, n] = total[QD : 2 * QD].astype(BF16)
            return carry

        lax.fori_loop(0, 4, body, 0)
        for y_ in (yh, oy):
            for cc in (0, 1):
                away, here, owner = x_copy(y_, zo, cc)
                if cc == 1:
                    away.start()
                else:

                    @pl.when(owner == x)
                    def _():
                        pltpu.make_async_copy(*here).start()

                    @pl.when(owner != x)
                    def _():
                        away.start()

    u = (z - 4 * (x % 2) + NZ) % NZ
    power = (1 + 3 * (u % 2)) * (1 + 15 * ((u // 2) % 2)) * (1 + 255 * (u // 4))

    def ranked(i):
        table = ((0, 1, 2, 3, 3, 3, 0, 0), (1, 0, 1, 2, 2, 2, 3, 1), (2, 2, 3, 1, 1, 0, 1, 2), (3, 3, 0, 0, 0, 1, 2, 3))[i]
        return (sum(v * 4**n for n, v in enumerate(table)) // power) % 4

    def add_x(i):
        zq = ranked(i)
        e = zq % 2
        for cc in (0, 1):
            for xs in range(4):
                ref = rx.at[xs, cc, zq]
                pltpu.make_async_copy(ref, ref, x_r.at[xs, cc, zq]).wait()
            total = rx[0, cc, zq].astype(F32)
            for xs in range(1, 4):
                total = total + rx[xs, cc, zq].astype(F32)

            @pl.when(zq // 2 == yl)
            def _():
                keep[e, cc] = total

            @pl.when(zq // 2 != yl)
            def _():
                ysend[e, cc] = total.astype(BF16)
                rdma(ysend.at[e, cc], ry.at[e, cc], f_s.at[e, cc], f_r.at[e, cc], beside).start()

    def proj_group(k, carry):
        for i in range(8):

            @pl.when(k == i)
            def _():
                before(ga, i, False)
                if i == 6:
                    add_x(0)

        project(group_z(k))
        return carry

    lax.fori_loop(0, 8, proj_group, 0)
    for i in (1, 2, 3):
        add_x(i)

    sends = [
        rdma(ysend.at[e, cc], ry.at[e, cc], f_s.at[e, cc], f_r.at[e, cc], beside)
        for e in (0, 1)
        for cc in (0, 1)
    ]
    k = 0
    for e in (0, 1):
        for cc in (0, 1):
            sends[k].wait_recv()
            k += 1
            for half in (0, 1):
                out_buf[(e * 2 + cc) * QD : (e * 2 + cc + 1) * QD, half * 256 : (half + 1) * 256] = (
                    keep[e, cc, half] + ry[e, cc, half].astype(F32)
                ).astype(BF16)
    proj_out = pltpu.make_async_copy(out_buf, out_hbm, out_sem.at[1])
    proj_out.start()

    for cp in sends:
        cp.wait_send()

    def x_done(k, carry):
        zo = group_z(k)
        for y_ in (yh, oy):
            for cc in (0, 1):
                away, here, owner = x_copy(y_, zo, cc)
                if cc == 1:
                    away.wait_send()
                else:

                    @pl.when(owner != x)
                    def _():
                        away.wait_send()

        return carry

    lax.fori_loop(0, 8, x_done, 0)
    gk.finish()
    ga.finish()
    att_out.wait()
    proj_out.wait()


def per_device(queries, new_keys, new_values, segment_ids, cache_keys, cache_values, cache_lengths, o_weight):
    any_ = pl.BlockSpec(memory_space=pl.ANY)
    vmem = pl.BlockSpec(memory_space=pltpu.VMEM)
    smem = pl.BlockSpec(memory_space=pltpu.SMEM)
    dma = pltpu.SemaphoreType.DMA
    att, out = pl.pallas_call(
        kernel,
        out_shape=(
            jax.ShapeDtypeStruct((ROWS, HD), BF16),
            jax.ShapeDtypeStruct((4 * QD, 512), BF16),
        ),
        in_specs=[any_, any_, any_, vmem, any_, any_, smem, any_],
        out_specs=(any_, any_),
        scratch_shapes=[
            pltpu.VMEM((2, 2, NZ, PKT, HD), BF16),
            pltpu.VMEM((ROWS, HD), BF16),
            pltpu.VMEM((ROWS, HD), F32),
            pltpu.VMEM((ROWS, HD), F32),
            pltpu.VMEM((ROWS, 2 * HD), F32),
            pltpu.VMEM((2, RCHUNK, 5 * CD), F32),
            pltpu.VMEM((2, RCHUNK, HD), F32),
            pltpu.VMEM((5 * CD, 2 * HD), BF16),
            pltpu.VMEM((4, HEADS * HD, 256), BF16),
            pltpu.VMEM((2, NZ, PAIRS, QD, 256), BF16),
            pltpu.VMEM((ROWS, HD), F32),
            pltpu.VMEM((ROWS, HD), BF16),
            pltpu.VMEM((2, NZ, 4, QD, 256), BF16),
            pltpu.VMEM((4, 2, 4, 2, QD, 256), BF16),
            pltpu.VMEM((2, 2, 2, QD, 256), F32),
            pltpu.VMEM((2, 2, 2, QD, 256), BF16),
            pltpu.VMEM((2, 2, 2, QD, 256), BF16),
            pltpu.VMEM((4 * QD, 512), BF16),
            dma((5,)), dma((2,)), dma((2,)),
            dma((2, 4, 3)), dma((2, 4, 3)), dma((10,)), dma((10,)), dma((4, 9)), dma((4, 9)),
            dma((2, 4, 3)), dma((2, 4, 3)), dma((10,)), dma((10,)),
            dma((2, NZ, 2)), dma((4, 2, 4)), dma((2, 2)), dma((2, 2)), dma((2,)), dma((2,)),
        ],
        compiler_params=pltpu.CompilerParams(
            collective_id=0, has_side_effects=True, vmem_limit_bytes=56 << 20
        ),
    )(
        queries.reshape(ROWS, HD),
        new_keys.reshape(QD, HD),
        new_values.reshape(QD, HD),
        segment_ids.reshape(1, QD),
        cache_keys.reshape(CD, HD),
        cache_values.reshape(CD, HD),
        cache_lengths,
        o_weight,
    )
    return att.reshape(QD, HEADS, HD), out


def solution(mesh):
    return jax.shard_map(
        per_device,
        mesh=mesh,
        in_specs=(
            P("blk", "head", None),
            P("blk", "head", None),
            P("blk", "head", None),
            P("blk"),
            P("blk", "head", None),
            P("blk", "head", None),
            P("blk"),
            P("head", "blk"),
        ),
        out_specs=(P("blk", "head", None), P("head", "blk")),
        check_vma=False,
    )
```

time: 140 us -> 104 us (0.74)
  the two profiles are of different devices: /device:TPU:95 before, /device:TPU:39 now
where the time goes in v2:
time: 104 us
  Pallas kernels  99.4 us (96%)
  local copies, waits for them, and re-layouts  3.34 us (3%)
  between operations  1.29 us (1%)
    pallas_call x1, Pallas kernels, per_device(): pl.pallas_call(kernel, out_shape=(jax.ShapeDtypeStruct((ROWS, HD), BF16),...  99.4 us
    unnamed x2, local copies, waits for them, and re-layouts  3.34 us

profile of v2, /device:TPU:39, one launch (start us, length us, event | category | flops | bytes accessed | tf_op | source)
XLA Modules:
  0.0 104.1 jit_solution(14655854003293170771)
XLA Ops:
  1.3 99.4 %shard_map.95 = (bf16[1024,128]{1,0:T(8,128)(2,1)}, bf16[256,512]{1,0:T(8,128)(2,1)}) custom-call(bf16[1024,128]{1,0:T(8,128)(2,1)} %bitcast.7, bf16[64,128]{1,0:T(8,128)(2,1)} %bitcast.11, bf16[64,128]{1,0:T(8,128)(2,1)} %bitcast.12, s32[1,64]{1,0:T(1,128)} %bitcast.13, bf16[256,128]{1,0:T(8,128)(2,1)} %bitcast.9, bf16[256,128]{1,0:T(8,128)(2,1)} %bitcast.10, ...), custom_call_target="tpu_custom_call" | custom-call | tf_op jit(solution)/shard_map/pallas_call | solution.py:508
  100.7 1.7 %copy.13 = bf16[64,16,128]{2,1,0:T(8,128)(2,1)} copy(bf16[64,16,128]{2,1,0:T(8,128)(2,1)} %bitcast.8) | data formatting | bytes 524288
  102.4 1.7 %copy.14 = bf16[256,512]{1,0:T(8,128)(2,1)} copy(bf16[256,512]{1,0:T(8,128)(2,1)} %get-tuple-element.9) | data formatting | bytes 524288

commit v3 on v2

--- a/solution.py
+++ b/solution.py
@@ -19,26 +19,27 @@
 ROWS = QD * HEADS
 NZ = 8
 KN0, VN0, META0, PKT = 2 * CD, 2 * CD + QD, 2 * CD + 2 * QD, 2 * CD + 2 * QD + 16
+HALF = QD // 2
 PAIRS = HEADS // 2
 LOW = -1e30
 SCALE = math.log2(math.e) / math.sqrt(HD)
 
-KP = 448
-KQ_MID = 560
-AP = 5
+KP = 336
+KQ_MID = 496
+AP = 4
 AQ_MID = 6
 
-RCHUNK = 256
+RCHUNK = 512
 
 
 def kernel(
     q_hbm, kn_hbm, vn_hbm, seg_ref, kc_hbm, vc_hbm, len_ref, w_hbm,
     att_hbm, out_hbm,
-    kv, q_buf, segq, m_buf, acc, sc, m_next, vb, w_buf, abuf, att_f32, att_bf, psend, rx, keep, ysend, ry, out_buf,
+    kv, q_buf, segq, m_buf, acc, sc, m_next, vb, w_buf, abuf, att_f32, att_bf, psend, relay, rx, keep, ysend, ry, out_buf,
     in_sem, w_sem, out_sem,
     kz_s, kz_r, ky_s, ky_r, kb_s, kb_r,
     az_s, az_r, ay_s, ay_r,
-    x_s, x_r, f_s, f_r, wx_s, wx_r,
+    x_s, x_r, r_r, f_s, f_r, wx_s, wx_r,
 ):
     b = lax.axis_index("blk")
     h = lax.axis_index("head")
@@ -63,7 +64,7 @@
 
     barrier = pltpu.get_barrier_semaphore()
     partners = [right, left, across, sibling, beside]
-    for dx in (1, 2, 3):
+    for dx in (1, 3):
         for cc in (0, 1):
             partners.append(dev(yh, z, cc, (x + dx) % 4, yl))
     for to in partners:
@@ -98,9 +99,10 @@
     pl.semaphore_wait(barrier, len(partners))
 
     class Gather:
-        def __init__(self, slot, p, qs, qa, qb, zs, zr, ys, yr, sib=None):
+        def __init__(self, slot, p, qs, qa, qb, zs, zr, ys, yr, sib=None, tail=None):
             self.slot, self.p, self.q, self.qa, self.qb = slot, p, qs, qa, qb
             self.zs, self.zr, self.ys, self.yr, self.sib = zs, zr, ys, yr, sib
+            self.tail = tail
             self.sent = []
 
         def go(self, copy):
@@ -111,23 +113,28 @@
             return (z + NZ - s) % NZ if d == 0 else (z + s) % NZ
 
         def part(self, kind, d, s):
+            if kind == 3:
+                return self.tail[1] if self.tail and s == 4 else None
             if kind < 2:
                 if s == 4 and kind != d:
                     return None
-                return self.p
+                return self.tail[0] if self.tail and s == 4 else self.p
             if s == 4:
                 return self.qa if d == 0 else self.qb
             return self.q
 
         def view(self, kind, d, s):
-            return self.slot(oy if kind == 1 else yh, self.z_of(d, s), self.part(kind, d, s))
+            return self.slot(self.plane(kind, d), self.z_of(d, s), self.part(kind, d, s))
+
+        def plane(self, kind, d):
+            return oy if kind == 1 or (kind == 3 and d == 1) else yh
 
         def z_send(self, kind, d, s):
             if self.part(kind, d, s) is None:
                 return
 
             def copy():
-                ref = self.slot(oy if kind == 1 else yh, self.z_of(d, s - 1), self.part(kind, d, s))
+                ref = self.slot(self.plane(kind, d), self.z_of(d, s - 1), self.part(kind, d, s))
                 return rdma(ref, ref, self.zs.at[d, s - 1, kind], self.zr.at[d, s - 1, kind], ring[d])
 
             self.go(copy)
@@ -216,6 +223,8 @@
                     self.z_wait(kind, d, s)
                     if s < 4:
                         self.z_send(kind, d, s + 1)
+                    if s == 3 and kind == d:
+                        self.z_send(3, d, 4)
                     if kind == 2:
                         self.y_send(d, s)
                     self.b_send(kind, d, s)
@@ -312,24 +321,23 @@
         return (z + (1 - 2 * (k % 2)) * s + NZ) % NZ
 
     def before(g, k, wait):
+        q_at = {0: 1, 1: 2, 2: 3, 4: 4}
+        if k in q_at:
+            g.forward((2,), q_at[k])
         if k == 0:
             g.middle()
             g.late(0)
-            g.forward((2,), 1)
             if wait:
                 g.b_wait(0, 0)
             return
         s = (k + 1) // 2
         if k % 2:
             g.forward((0, 1), s)
-            g.late(s)
-            if wait:
-                g.b_wait(0, s)
-                if s == 4:
-                    g.b_wait(1, s)
-        else:
-            g.forward((2,), s + 1)
-            if wait:
+        if k in (1, 3, 5, 6):
+            g.late((k + 2) // 2)
+        if wait:
+            g.b_wait(1 - k % 2, s)
+            if s == 4:
                 g.b_wait(1, s)
 
     def weights(i):
@@ -367,9 +375,9 @@
         ].astype(BF16)
 
     ga = Gather(
-        lambda y_, z_, pc: abuf.at[y_, z_, pl.ds(pc[0], pc[1])],
+        lambda y_, z_, pc: abuf.at[y_, z_, pl.ds(pc[0], pc[1]), pl.ds(pc[2] if len(pc) > 2 else 0, QD // 2 if len(pc) > 2 else QD)],
         (0, AP), (AP, PAIRS - AP), (AP, AQ_MID - AP), (AQ_MID, PAIRS - AQ_MID),
-        az_s, az_r, ay_s, ay_r,
+        az_s, az_r, ay_s, ay_r, None, ((0, AP, 0), (0, AP, QD // 2)),
     )
     ga.open()
     att_out = pltpu.make_async_copy(att_bf, att_hbm, out_sem.at[0])
@@ -378,42 +386,78 @@
         for cp in weights(i):
             cp.wait()
 
-    def x_copy(y_, z_, cc):
-        to_c = c if cc == 0 else oc
-        owner = 2 * y_ + z_ // 4
-        src = psend.at[y_, z_, pl.ds(2 * to_c, 2)]
-        dst = rx.at[x, c, z_ % 4]
-        rs = x_r.at[x, c, z_ % 4]
-        away = rdma(src, dst, x_s.at[y_, z_, cc], rs, dev(yh, z, to_c, owner, yl))
-        return away, (src, dst, rs), owner
-
-    def project(zo):
+    def rows_of(hf):
+        return pl.ds(hf * HALF, HALF)
+
+    def to_self(zo, hf):
+        return rdma(
+            psend.at[x // 2, zo, pl.ds(2 * oc, 2), rows_of(hf)],
+            rx.at[2, c, zo % 4, :, rows_of(hf)],
+            x_s.at[zo, hf, 0], x_r.at[2, c, zo % 4, hf], sibling,
+        )
+
+    def to_relay(zo, hf):
+        via = (x + (1 if hf == 0 else 3)) % 4
+        return rdma(
+            psend.at[1 - x // 2, zo, :, rows_of(hf)],
+            relay.at[zo % 4, hf],
+            x_s.at[zo, hf, 1], r_r.at[zo % 4, hf], dev(yh, z, c, via, yl),
+        )
+
+    def to_owner(zo, hf, up, other):
+        owner = (x + (1 if up else 3)) % 4
+        to_c = oc if other else c
+        relayed = (hf == 0) == up
+        return rdma(
+            psend.at[owner // 2, zo, pl.ds(2 * to_c, 2), rows_of(hf)],
+            rx.at[0 if up else 1, c, zo % 4, :, rows_of(hf)],
+            x_s.at[zo, hf, 2 * relayed + other], x_r.at[0 if up else 1, c, zo % 4, hf],
+            dev(yh, z, to_c, owner, yl),
+        )
+
+    def send_x(zo, halves):
+        @pl.when(zo // 4 == x % 2)
+        def _():
+            for hf in halves:
+                to_relay(zo, hf).start()
+                to_self(zo, hf).start()
+
+        @pl.when(zo // 4 != x % 2)
+        def _():
+            for hf in halves:
+                for other in (0, 1):
+                    to_owner(zo, hf, hf == 1, other).start()
+
+    def relay_x(zo, halves):
+        @pl.when(zo // 4 != x % 2)
+        def _():
+            for hf in halves:
+                to_relay(zo, hf).wait_recv()
+                y_ = ((x + (1 if hf == 0 else 3)) % 4) // 2
+                mine = psend.at[y_, zo]
+                rows = slice(hf * HALF, (hf + 1) * HALF)
+                mine[:, rows] = (mine[:, rows].astype(F32) + relay[zo % 4, hf].astype(F32)).astype(BF16)
+                for other in (0, 1):
+                    to_owner(zo, hf, hf == 0, other).start()
+
+    def project(zo, halves):
+        first, count = halves[0] * HALF, len(halves) * HALF
+
         def body(n, carry):
-            total = jnp.zeros((2 * QD, 256), F32)
+            total = jnp.zeros((2 * count, 256), F32)
             for j in range(PAIRS):
-                lhs = jnp.concatenate([abuf[yh, zo, j], abuf[oy, zo, j]], axis=0)
+                lhs = jnp.concatenate(
+                    [abuf[yh, zo, j, first : first + count], abuf[oy, zo, j, first : first + count]], axis=0
+                )
                 total = total + jnp.dot(
                     lhs, w_buf[n, j * 256 : (j + 1) * 256, :], preferred_element_type=F32
                 )
-            psend[yh, zo, n] = total[0:QD].astype(BF16)
-            psend[oy, zo, n] = total[QD : 2 * QD].astype(BF16)
+            psend[yh, zo, n, first : first + count] = total[0:count].astype(BF16)
+            psend[oy, zo, n, first : first + count] = total[count : 2 * count].astype(BF16)
             return carry
 
         lax.fori_loop(0, 4, body, 0)
-        for y_ in (yh, oy):
-            for cc in (0, 1):
-                away, here, owner = x_copy(y_, zo, cc)
-                if cc == 1:
-                    away.start()
-                else:
-
-                    @pl.when(owner == x)
-                    def _():
-                        pltpu.make_async_copy(*here).start()
-
-                    @pl.when(owner != x)
-                    def _():
-                        away.start()
+        send_x(zo, halves)
 
     u = (z - 4 * (x % 2) + NZ) % NZ
     power = (1 + 3 * (u % 2)) * (1 + 15 * ((u // 2) % 2)) * (1 + 255 * (u // 4))
@@ -422,78 +466,112 @@
         table = ((0, 1, 2, 3, 3, 3, 0, 0), (1, 0, 1, 2, 2, 2, 3, 1), (2, 2, 3, 1, 1, 0, 1, 2), (3, 3, 0, 0, 0, 1, 2, 3))[i]
         return (sum(v * 4**n for n, v in enumerate(table)) // power) % 4
 
-    def add_x(i):
+    def y_copy(e, cc, hf):
+        rows = pl.ds(hf * HALF, HALF)
+        return rdma(
+            ysend.at[e, cc, :, rows], ry.at[e, cc, :, rows], f_s.at[e, cc, hf], f_r.at[e, cc, hf], beside
+        )
+
+    def add_x(i, halves):
         zq = ranked(i)
         e = zq % 2
-        for cc in (0, 1):
-            for xs in range(4):
-                ref = rx.at[xs, cc, zq]
-                pltpu.make_async_copy(ref, ref, x_r.at[xs, cc, zq]).wait()
-            total = rx[0, cc, zq].astype(F32)
-            for xs in range(1, 4):
-                total = total + rx[xs, cc, zq].astype(F32)
+        first, count = halves[0] * HALF, len(halves) * HALF
+        rows = slice(first, first + count)
+        for cc in (c, oc):
+            for side in (0, 1) if cc is c else (0, 1, 2):
+                for hf in halves:
+                    ref = rx.at[side, cc, zq, :, rows_of(hf)]
+                    pltpu.make_async_copy(ref, ref, x_r.at[side, cc, zq, hf]).wait()
+            if cc is c:
+                total = psend[x // 2, 4 * (x % 2) + zq, pl.ds(2 * c, 2), rows].astype(F32)
+            else:
+                total = rx[2, cc, zq, :, rows].astype(F32)
+            for side in (0, 1):
+                total = total + rx[side, cc, zq, :, rows].astype(F32)
 
             @pl.when(zq // 2 == yl)
             def _():
-                keep[e, cc] = total
+                keep[e, cc, :, rows] = total
 
             @pl.when(zq // 2 != yl)
             def _():
-                ysend[e, cc] = total.astype(BF16)
-                rdma(ysend.at[e, cc], ry.at[e, cc], f_s.at[e, cc], f_r.at[e, cc], beside).start()
+                ysend[e, cc, :, rows] = total.astype(BF16)
+                for hf in halves:
+                    y_copy(e, cc, hf).start()
+
+    def add_y(i):
+        zq = ranked(i)
+        e = zq % 2
+
+        @pl.when(zq // 2 == yl)
+        def _():
+            for hf in (0, 1):
+                for cc in (0, 1):
+                    y_copy(e, cc, hf).wait_recv()
+                    rows = pl.ds(pl.multiple_of(e * 2 * QD + cc * QD + hf * HALF, HALF), HALF)
+                    part = slice(hf * HALF, (hf + 1) * HALF)
+                    for half in (0, 1):
+                        out_buf[rows, half * 256 : (half + 1) * 256] = (
+                            keep[e, cc, half, part] + ry[e, cc, half, part].astype(F32)
+                        ).astype(BF16)
 
     def proj_group(k, carry):
-        for i in range(8):
+        for i in range(7):
 
             @pl.when(k == i)
             def _():
                 before(ga, i, False)
-                if i == 6:
-                    add_x(0)
-
-        project(group_z(k))
+
+
+        project(group_z(k), (0, 1))
+        for i in range(1, 7):
+
+            @pl.when(k == i)
+            def _():
+                relay_x(group_z(i - 1), (0, 1))
+
         return carry
 
-    lax.fori_loop(0, 8, proj_group, 0)
-    for i in (1, 2, 3):
-        add_x(i)
-
-    sends = [
-        rdma(ysend.at[e, cc], ry.at[e, cc], f_s.at[e, cc], f_r.at[e, cc], beside)
-        for e in (0, 1)
-        for cc in (0, 1)
-    ]
-    k = 0
+    lax.fori_loop(0, 7, proj_group, 0)
+    last = group_z(7)
+    ga.forward((0, 1), 4)
+    project(last, (0,))
+    relay_x(group_z(6), (0, 1))
+    ga.forward((3,), 4)
+    project(last, (1,))
+    relay_x(last, (0,))
+    relay_x(last, (1,))
+    for i in (0, 1, 2):
+        add_x(i, (0, 1))
+    for hf in (0, 1):
+        add_x(3, (hf,))
+    for i in range(4):
+        add_y(i)
+    proj_out = pltpu.make_async_copy(out_buf, out_hbm, out_sem.at[1])
+    proj_out.start()
+
     for e in (0, 1):
         for cc in (0, 1):
-            sends[k].wait_recv()
-            k += 1
-            for half in (0, 1):
-                out_buf[(e * 2 + cc) * QD : (e * 2 + cc + 1) * QD, half * 256 : (half + 1) * 256] = (
-                    keep[e, cc, half] + ry[e, cc, half].astype(F32)
-                ).astype(BF16)
-    proj_out = pltpu.make_async_copy(out_buf, out_hbm, out_sem.at[1])
-    proj_out.start()
-
-    for cp in sends:
-        cp.wait_send()
-
-    def x_done(k, carry):
-        zo = group_z(k)
-        for y_ in (yh, oy):
-            for cc in (0, 1):
-                away, here, owner = x_copy(y_, zo, cc)
-                if cc == 1:
-                    away.wait_send()
-                else:
-
-                    @pl.when(owner != x)
-                    def _():
-                        away.wait_send()
+            for hf in (0, 1):
+                y_copy(e, cc, hf).wait_send()
+
+    def x_done(zo, carry):
+        @pl.when(zo // 4 == x % 2)
+        def _():
+            for hf in (0, 1):
+                to_relay(zo, hf).wait_send()
+                to_self(zo, hf).wait_send()
+
+        @pl.when(zo // 4 != x % 2)
+        def _():
+            for hf in (0, 1):
+                for up in (False, True):
+                    for other in (0, 1):
+                        to_owner(zo, hf, up, other).wait_send()
 
         return carry
 
-    lax.fori_loop(0, 8, x_done, 0)
+    lax.fori_loop(0, NZ, x_done, 0)
     gk.finish()
     ga.finish()
     att_out.wait()
@@ -527,15 +605,16 @@
             pltpu.VMEM((ROWS, HD), F32),
             pltpu.VMEM((ROWS, HD), BF16),
             pltpu.VMEM((2, NZ, 4, QD, 256), BF16),
-            pltpu.VMEM((4, 2, 4, 2, QD, 256), BF16),
+            pltpu.VMEM((4, 2, 4, HALF, 256), BF16),
+            pltpu.VMEM((3, 2, 4, 2, QD, 256), BF16),
             pltpu.VMEM((2, 2, 2, QD, 256), F32),
             pltpu.VMEM((2, 2, 2, QD, 256), BF16),
             pltpu.VMEM((2, 2, 2, QD, 256), BF16),
             pltpu.VMEM((4 * QD, 512), BF16),
             dma((5,)), dma((2,)), dma((2,)),
             dma((2, 4, 3)), dma((2, 4, 3)), dma((10,)), dma((10,)), dma((4, 9)), dma((4, 9)),
-            dma((2, 4, 3)), dma((2, 4, 3)), dma((10,)), dma((10,)),
-            dma((2, NZ, 2)), dma((4, 2, 4)), dma((2, 2)), dma((2, 2)), dma((2,)), dma((2,)),
+            dma((2, 4, 4)), dma((2, 4, 4)), dma((10,)), dma((10,)),
+            dma((NZ, 2, 4)), dma((3, 2, 4, 2)), dma((4, 2)), dma((2, 2, 2)), dma((2, 2, 2)), dma((2,)), dma((2,)),
         ],
         compiler_params=pltpu.CompilerParams(
             collective_id=0, has_side_effects=True, vmem_limit_bytes=56 << 20

time: 104 us -> 95.4 us (0.917)
  the two profiles are of different devices: /device:TPU:39 before, /device:TPU:2 now
where the time goes in v3:
time: 95.4 us; the launch traced here: 95.2 us
  Pallas kernels  90.6 us (95%)
  local copies, waits for them, and re-layouts  3.34 us (4%)
  between operations  1.29 us (1%)
    pallas_call x1, Pallas kernels, per_device(): pl.pallas_call(kernel, out_shape=(jax.ShapeDtypeStruct((ROWS, HD), BF16),...  90.6 us
    unnamed x2, local copies, waits for them, and re-layouts  3.34 us

profile of v3, /device:TPU:2, one launch (start us, length us, event | category | flops | bytes accessed | tf_op | source)
XLA Modules:
  0.0 95.2 jit_solution(14751907257757790987)
XLA Ops:
  1.3 90.6 %shard_map.95 = (bf16[1024,128]{1,0:T(8,128)(2,1)}, bf16[256,512]{1,0:T(8,128)(2,1)}) custom-call(bf16[1024,128]{1,0:T(8,128)(2,1)} %bitcast.7, bf16[64,128]{1,0:T(8,128)(2,1)} %bitcast.11, bf16[64,128]{1,0:T(8,128)(2,1)} %bitcast.12, s32[1,64]{1,0:T(1,128)} %bitcast.13, bf16[256,128]{1,0:T(8,128)(2,1)} %bitcast.9, bf16[256,128]{1,0:T(8,128)(2,1)} %bitcast.10, ...), custom_call_target="tpu_custom_call" | custom-call | tf_op jit(solution)/shard_map/pallas_call | solution.py:586
  91.8 1.7 %copy.13 = bf16[64,16,128]{2,1,0:T(8,128)(2,1)} copy(bf16[64,16,128]{2,1,0:T(8,128)(2,1)} %bitcast.8) | data formatting | bytes 524288
  93.5 1.7 %copy.14 = bf16[256,512]{1,0:T(8,128)(2,1)} copy(bf16[256,512]{1,0:T(8,128)(2,1)} %get-tuple-element.9) | data formatting | bytes 524288

commit v4 on v3

--- a/solution.py
+++ b/solution.py
@@ -320,25 +320,25 @@
         s = (k + 1) // 2
         return (z + (1 - 2 * (k % 2)) * s + NZ) % NZ
 
-    def before(g, k, wait):
+    def arrived(g, k):
+        s = (k + 1) // 2
+        g.b_wait(0 if s == 0 else 1 - k % 2, s)
+        if s == 4:
+            g.b_wait(1, s)
+
+    def before(g, k):
         q_at = {0: 1, 1: 2, 2: 3, 4: 4}
         if k in q_at:
             g.forward((2,), q_at[k])
         if k == 0:
             g.middle()
             g.late(0)
-            if wait:
-                g.b_wait(0, 0)
             return
         s = (k + 1) // 2
         if k % 2:
             g.forward((0, 1), s)
         if k in (1, 3, 5, 6):
             g.late((k + 2) // 2)
-        if wait:
-            g.b_wait(1 - k % 2, s)
-            if s == 4:
-                g.b_wait(1, s)
 
     def weights(i):
         half = w_hbm.at[:, pl.ds(i * 256, 256)]
@@ -347,19 +347,25 @@
         return here, rdma(half, slot, wx_s.at[i], wx_r.at[i], sibling)
 
     def kv_group(k, carry):
-        for i in range(8):
+        for i in range(9):
 
             @pl.when(k == i)
             def _():
-                before(gk, i, True)
+                if i < 8:
+                    before(gk, i)
+                if i > 0:
+                    arrived(gk, i - 1)
                 if i in (2, 3):
                     for cp in weights(i - 2):
                         cp.start()
 
-        attend(group_z(k))
+        @pl.when(k > 0)
+        def _():
+            attend(group_z(k - 1))
+
         return carry
 
-    lax.fori_loop(0, 8, kv_group, 0)
+    lax.fori_loop(0, 9, kv_group, 0)
 
     def finish_rows(r, carry):
         rows = pl.ds(pl.multiple_of(r * RCHUNK, RCHUNK), RCHUNK)
@@ -520,7 +526,7 @@
 
             @pl.when(k == i)
             def _():
-                before(ga, i, False)
+                before(ga, i)
 
 
         project(group_z(k), (0, 1))
@@ -536,13 +542,14 @@
     last = group_z(7)
     ga.forward((0, 1), 4)
     project(last, (0,))
+    add_x(0, (0, 1))
     relay_x(group_z(6), (0, 1))
     ga.forward((3,), 4)
     project(last, (1,))
     relay_x(last, (0,))
+    add_x(1, (0, 1))
     relay_x(last, (1,))
-    for i in (0, 1, 2):
-        add_x(i, (0, 1))
+    add_x(2, (0, 1))
     for hf in (0, 1):
         add_x(3, (hf,))
     for i in range(4):

time: 95.4 us -> 93.1 us (0.976)
  Pallas kernels: 90.6 us -> 88.3 us
    pallas_call x1, Pallas kernels: 90.6 us -> 88.3 us  [per_device(): pl.pallas_call(kernel, out_shape=(jax.ShapeDtypeStruct((ROWS, HD), BF16),...]
where the time goes in v4:
time: 93.1 us; the launch traced here: 93 us
  Pallas kernels  88.3 us (95%)
  local copies, waits for them, and re-layouts  3.34 us (4%)
  between operations  1.29 us (1%)
    pallas_call x1, Pallas kernels, per_device(): pl.pallas_call(kernel, out_shape=(jax.ShapeDtypeStruct((ROWS, HD), BF16),...  88.3 us
    unnamed x2, local copies, waits for them, and re-layouts  3.34 us

profile of v4, /device:TPU:2, one launch (start us, length us, event | category | flops | bytes accessed | tf_op | source)
XLA Modules:
  0.0 93.0 jit_solution(17737817379779289114)
XLA Ops:
  1.3 88.3 %shard_map.95 = (bf16[1024,128]{1,0:T(8,128)(2,1)}, bf16[256,512]{1,0:T(8,128)(2,1)}) custom-call(bf16[1024,128]{1,0:T(8,128)(2,1)} %bitcast.7, bf16[64,128]{1,0:T(8,128)(2,1)} %bitcast.11, bf16[64,128]{1,0:T(8,128)(2,1)} %bitcast.12, s32[1,64]{1,0:T(1,128)} %bitcast.13, bf16[256,128]{1,0:T(8,128)(2,1)} %bitcast.9, bf16[256,128]{1,0:T(8,128)(2,1)} %bitcast.10, ...), custom_call_target="tpu_custom_call" | custom-call | tf_op jit(solution)/shard_map/pallas_call | solution.py:593
  89.6 1.7 %copy.13 = bf16[64,16,128]{2,1,0:T(8,128)(2,1)} copy(bf16[64,16,128]{2,1,0:T(8,128)(2,1)} %bitcast.8) | data formatting | bytes 524288
  91.3 1.7 %copy.14 = bf16[256,512]{1,0:T(8,128)(2,1)} copy(bf16[256,512]{1,0:T(8,128)(2,1)} %get-tuple-element.9) | data formatting | bytes 524288

commit v5 on v4

--- a/solution.py
+++ b/solution.py
@@ -539,16 +539,37 @@
         return carry
 
     lax.fori_loop(0, 7, proj_group, 0)
+    def x_done(k, carry):
+        zo = group_z(k)
+
+        @pl.when(zo // 4 == x % 2)
+        def _():
+            for hf in (0, 1):
+                to_relay(zo, hf).wait_send()
+                to_self(zo, hf).wait_send()
+
+        @pl.when(zo // 4 != x % 2)
+        def _():
+            for hf in (0, 1):
+                for up in (False, True):
+                    for other in (0, 1):
+                        to_owner(zo, hf, up, other).wait_send()
+
+        return carry
+
     last = group_z(7)
     ga.forward((0, 1), 4)
     project(last, (0,))
     add_x(0, (0, 1))
     relay_x(group_z(6), (0, 1))
+    gk.finish()
     ga.forward((3,), 4)
     project(last, (1,))
     relay_x(last, (0,))
     add_x(1, (0, 1))
     relay_x(last, (1,))
+    ga.finish()
+    lax.fori_loop(0, 6, x_done, 0)
     add_x(2, (0, 1))
     for hf in (0, 1):
         add_x(3, (hf,))
@@ -562,25 +583,7 @@
             for hf in (0, 1):
                 y_copy(e, cc, hf).wait_send()
 
-    def x_done(zo, carry):
-        @pl.when(zo // 4 == x % 2)
-        def _():
-            for hf in (0, 1):
-                to_relay(zo, hf).wait_send()
-                to_self(zo, hf).wait_send()
-
-        @pl.when(zo // 4 != x % 2)
-        def _():
-            for hf in (0, 1):
-                for up in (False, True):
-                    for other in (0, 1):
-                        to_owner(zo, hf, up, other).wait_send()
-
-        return carry
-
-    lax.fori_loop(0, NZ, x_done, 0)
-    gk.finish()
-    ga.finish()
+    lax.fori_loop(6, 8, x_done, 0)
     att_out.wait()
     proj_out.wait()
 

time: 93.1 us -> 93.2 us (level)
  no operation moved by 1% of the time
where the time goes in v5:
time: 93.2 us; the launch traced here: 93.1 us
  Pallas kernels  88.4 us (95%)
  local copies, waits for them, and re-layouts  3.34 us (4%)
  between operations  1.29 us (1%)
    pallas_call x1, Pallas kernels, per_device(): pl.pallas_call(kernel, out_shape=(jax.ShapeDtypeStruct((ROWS, HD), BF16),...  88.4 us
    unnamed x2, local copies, waits for them, and re-layouts  3.34 us

profile of v5, /device:TPU:2, one launch (start us, length us, event | category | flops | bytes accessed | tf_op | source)
XLA Modules:
  0.0 93.1 jit_solution(1380017289996985550)
XLA Ops:
  1.3 88.4 %shard_map.95 = (bf16[1024,128]{1,0:T(8,128)(2,1)}, bf16[256,512]{1,0:T(8,128)(2,1)}) custom-call(bf16[1024,128]{1,0:T(8,128)(2,1)} %bitcast.7, bf16[64,128]{1,0:T(8,128)(2,1)} %bitcast.11, bf16[64,128]{1,0:T(8,128)(2,1)} %bitcast.12, s32[1,64]{1,0:T(1,128)} %bitcast.13, bf16[256,128]{1,0:T(8,128)(2,1)} %bitcast.9, bf16[256,128]{1,0:T(8,128)(2,1)} %bitcast.10, ...), custom_call_target="tpu_custom_call" | custom-call | tf_op jit(solution)/shard_map/pallas_call | solution.py:596
  89.7 1.7 %copy.13 = bf16[64,16,128]{2,1,0:T(8,128)(2,1)} copy(bf16[64,16,128]{2,1,0:T(8,128)(2,1)} %bitcast.8) | data formatting | bytes 524288
  91.4 1.7 %copy.14 = bf16[256,512]{1,0:T(8,128)(2,1)} copy(bf16[256,512]{1,0:T(8,128)(2,1)} %get-tuple-element.9) | data formatting | bytes 524288
